TPU v7x, 256 devices: a whole 4x4x8 slice. The times are simulated.
256 devices in a mesh: outer: 16 (over y, z_hi), inner: 16 (over x, z_lo, core).
Axes of the slice: x: 4, y: 4, z: 8 (z_hi: 4, z_lo: 2; z = z_hi * 2 + z_lo), core: 2. Of those that a mesh axis runs over, the one named last changes fastest.
Arguments:
- hidden: bfloat16 [32768, 1024], P(('outer', 'inner')), may hold values from -24 to 24
- x_act: bfloat16 [32768, 2048], P(('outer', 'inner')), may hold values from -6 to 6
- dt_step: float32 [32768, 32], P(('outer', 'inner')), may hold values from 0.0014915534 to 0.44, as said below
- log_decay: float32 [32768, 32], P(('outer', 'inner')), may hold values from -0.81 to -8.85009766e-07, as said below
- w_bc: bfloat16 [1024, 128], P(('outer', 'inner')), may hold values from -0.1875 to 0.1875
- grad_y: bfloat16 [32768, 2048], P(('outer', 'inner')), may hold values from -0.19921875 to 0.19921875
Outputs:
- grad_x: float32 [32768, 2048], P(('outer', 'inner'))
- grad_hidden: float32 [32768, 1024], P(('outer', 'inner'))
- grad_proj: float32 [1024, 128], P(('outer', 'inner'))
Inputs may be any that keep to these rules, and one draw needn't show every extreme that they name: `dt_step`: Positive; constant in scale within each head apart from a factor within e**-0.5 to e**0.5. `log_decay`: Negative.
All inputs are finite; a program needn't handle non-finite values.
Results may differ from a plain program's by a relative error of at most 0.0029.
Values may be sent and summed in bfloat16 or wider, within the bound.
A program may use at most 64 MiB of HBM per device.

v0:
```python
import math
import jax
import jax.numpy as jnp
from jax import lax
from jax.sharding import PartitionSpec as P

BLOCK = 128
HIGH = lax.Precision.HIGHEST


def shifted(value, axis, steps):
    count = lax.axis_size(axis)
    first, last = (max(0, -steps), min(count, count - steps))
    return lax.ppermute(value, axis, [(source, source + steps) for source in range(first, last)])


def block_step(carried, pieces):
    inputs, decays, b_rows, c_rows = pieces
    length = inputs.shape[0]
    running = jnp.cumsum(decays, axis=0)
    row_ids = lax.broadcasted_iota(jnp.int32, (length, length), 0)
    col_ids = lax.broadcasted_iota(jnp.int32, (length, length), 1)
    causal = row_ids >= col_ids
    spread = running.T[:, :, None] - running.T[:, None, :]
    segment = jnp.where(causal[None], jnp.exp(jnp.where(causal[None], spread, 0.0)), 0.0)
    scores = jnp.einsum("in,jn->ij", c_rows, b_rows, precision=HIGH)
    outputs = jnp.einsum("hij,jhp->ihp", segment * scores[None], inputs, precision=HIGH)
    outputs = outputs + jnp.exp(running)[:, :, None] * jnp.einsum(
        "in,hpn->ihp", c_rows, carried, precision=HIGH
    )
    final_sum = running[-1]
    weights = jnp.exp(final_sum[None, :] - running)
    updated = jnp.exp(final_sum)[:, None, None] * carried + jnp.einsum(
        "jhp,jn->hpn", inputs * weights[:, :, None], b_rows, precision=HIGH
    )
    return (updated, outputs)


def scan_block(inputs, decays, b_rows, c_rows, carried, length):
    count = inputs.shape[0] // length
    pieces = (
        inputs.reshape((count, length) + inputs.shape[1:]),
        decays.reshape((count, length, decays.shape[1])),
        b_rows.reshape((count, length, b_rows.shape[1])),
        c_rows.reshape((count, length, c_rows.shape[1])),
    )
    final_state, outputs = lax.scan(block_step, carried, pieces)
    return (outputs.reshape(inputs.shape), final_state)


def combine(earlier, later):
    return (earlier[0] + later[0], jnp.exp(later[0])[:, None, None] * earlier[1] + later[1])


def doubling_prefix(own, backward):
    device_count = lax.axis_size(("outer", "inner"))
    distances = [1]
    reach = 1
    while reach < device_count:
        distances.append(reach)
        reach = reach * 2
    gathered = own
    for number, distance in enumerate(distances):
        if backward:
            arrived = shifted((gathered[0], gathered[1]), ("outer", "inner"), -distance)
        else:
            arrived = shifted((gathered[0], gathered[1]), ("outer", "inner"), distance)
        if number == 0:
            gathered = arrived
        else:
            gathered = combine(arrived, gathered)
    return gathered


def per_device(hidden, x_act, dt_step, log_decay, w_bc, grad_y):
    weights_full = lax.all_gather(w_bc, ("outer", "inner"), axis=0, tiled=True)
    state_width = weights_full.shape[1] // 2
    row_count = hidden.shape[0]
    head_count = dt_step.shape[1]
    head_size = x_act.shape[1] // head_count
    projected = jnp.dot(hidden, weights_full, preferred_element_type=jnp.float32)
    b_rows = projected[:, :state_width]
    c_rows = projected[:, state_width:]
    inputs = dt_step[:, :, None] * x_act.astype(jnp.float32).reshape(
        row_count, head_count, head_size
    )
    cotangent = grad_y.astype(jnp.float32).reshape(row_count, head_count, head_size)
    running = jnp.cumsum(log_decay, axis=0)
    totals = running[-1]
    own_state = jnp.einsum(
        "jhp,jn->hpn",
        inputs * jnp.exp(totals[None, :] - running)[:, :, None],
        b_rows,
        precision=HIGH,
    )
    own_adjoint = jnp.einsum(
        "ihp,in->hpn", cotangent * jnp.exp(running)[:, :, None], c_rows, precision=HIGH
    )
    state_in = doubling_prefix((totals, own_state), False)[1]
    adjoint_out = doubling_prefix((totals, own_adjoint), True)[1]

    def forward(inputs, b_rows, c_rows):
        return scan_block(inputs, log_decay, b_rows, c_rows, state_in, BLOCK)

    outputs, pullback = jax.vjp(forward, inputs, b_rows, c_rows)
    d_in, d_b, d_c = pullback((cotangent, adjoint_out))
    grad_x = (dt_step[:, :, None] * d_in).reshape(row_count, head_count * head_size)
    d_proj = jnp.concatenate([d_b, d_c], axis=1)
    d_low = d_proj.astype(jnp.bfloat16)
    grad_hidden = lax.dot_general(
        d_low, weights_full, (((1,), (1,)), ((), ())), preferred_element_type=jnp.float32
    )
    scale = 1.0 / math.sqrt(row_count * lax.axis_size("outer") * lax.axis_size("inner"))
    grad_proj = lax.psum_scatter(
        lax.dot_general(hidden, d_low, (((0,), (0,)), ((), ())), preferred_element_type=jnp.float32)
        * scale,
        ("outer", "inner"),
        scatter_dimension=0,
        tiled=True,
    )
    return (grad_x, grad_hidden, grad_proj)


def solution(mesh):
    in_specs = (
        P(("outer", "inner"), None),
        P(("outer", "inner"), None),
        P(("outer", "inner"), None),
        P(("outer", "inner"), None),
        P(("outer", "inner"), None),
        P(("outer", "inner"), None),
    )
    out_specs = (
        P(("outer", "inner"), None),
        P(("outer", "inner"), None),
        P(("outer", "inner"), None),
    )
    return jax.shard_map(
        per_device, mesh=mesh, in_specs=in_specs, out_specs=out_specs, check_vma=False
    )
```

profile of v0, /device:TPU:2, one launch (start us, length us, event | category | flops | bytes accessed | tf_op | source)
XLA Modules:
  0.0 1107.1 jit_solution(5641933597297097670)
XLA Ops:
  8.3 3.2 collective-permute-start
  11.5 1.9 collective-permute-start.17
  13.6 343.6 %all-gather = bf16[256,4,128]{2,1,0:T(4,128)(2,1)S(1)} all-gather(bf16[1,4,128]{2,1,0:T(4,128)(2,1)} %bitcast.65), channel_id=1, replica_groups=mesh['outer'=16,'inner'=16] {'outer','inner'}, dimensions={0}, use_global_device_ids=true | all-gather | bytes 263168 | tf_op jit(solution)/shard_map/all_gather | solution.py:76
  357.7 2.0 fusion.19
  359.7 3.2 collective-permute-start.8
  363.1 2.0 fusion.22
  365.1 1.9 collective-permute-start.25
  367.1 2.5 fusion
  371.9 3.5 fusion.3
  375.4 4.5 collective-permute-start.1
  380.0 1.9 collective-permute-start.18
  382.2 12.4 %collective-permute-start.2 = (f32[32]{0:T(128)S(1)}, f32[32]{0:T(128)S(1)}, u32[]{:S(2)}, u32[]{:S(2)}) collective-permute-start(f32[32]{0:T(128)S(1)} %get-tuple-element.192), channel_id=1, source_target_pairs={{2,0},{3,1},{4,2},{5,3},{6,4},{7,5},{8,6},{9,7},{10,8},{11,9},{12,... | collective-permute-start | bytes 392 | tf_op jit(solution)/shard_map/ppermute | solution.py:14
  394.6 1.9 collective-permute-start.19
  396.6 2.5 collective-permute-start.3
  399.1 1.9 collective-permute-done.19
  401.0 1.9 collective-permute-start.20
  402.9 2.5 collective-permute-start.9
  406.8 6.1 collective-permute-start.21
  412.9 1.9 collective-permute-start.26
  416.1 4.0 collective-permute-done.9
  420.1 1.4 multiply_add_fusion.14
  421.6 3.3 collective-permute-start.10
  424.8 11.8 %collective-permute-done.26 = f32[32,64,64]{2,1,0:T(8,128)S(1)} collective-permute-done((f32[32,64,64]{2,1,0:T(8,128)S(1)}, f32[32,64,64]{2,1,0:T(8,128)S(1)}, u32[]{:S(2)}, u32[]{:S(2)}) %collective-permute-start.26) | collective-permute-done | bytes 524320 | tf_op jit(solution)/shard_map/ppermute | solution.py:14
  436.8 1.9 collective-permute-start.27
  440.1 9.5 collective-permute-done.10
  449.7 1.9 collective-permute-start.11
  451.7 42.2 %collective-permute-done.27 = f32[32,64,64]{2,1,0:T(8,128)S(1)} collective-permute-done((f32[32,64,64]{2,1,0:T(8,128)S(1)}, f32[32,64,64]{2,1,0:T(8,128)S(1)}, u32[]{:S(2)}, u32[]{:S(2)}) %collective-permute-start.27) | collective-permute-done | bytes 524320 | tf_op jit(solution)/shard_map/ppermute | solution.py:14
  494.0 1.9 collective-permute-start.28
  498.7 22.1 %collective-permute-done.28 = f32[32,64,64]{2,1,0:T(8,128)S(1)} collective-permute-done((f32[32,64,64]{2,1,0:T(8,128)S(1)}, f32[32,64,64]{2,1,0:T(8,128)S(1)}, u32[]{:S(2)}, u32[]{:S(2)}) %collective-permute-start.28) | collective-permute-done | bytes 524320 | tf_op jit(solution)/shard_map/ppermute | solution.py:14
  521.0 20.4 %collective-permute-start.29 = (f32[32,64,64]{2,1,0:T(8,128)S(1)}, f32[32,64,64]{2,1,0:T(8,128)S(1)}, u32[]{:S(2)}, u32[]{:S(2)}) collective-permute-start(f32[32,64,64]{2,1,0:T(8,128)S(1)} %multiply_add_fusion.4), channel_id=1, source_target_pairs={{0,8},{1,9},{2,10},{3,11},{4,12},{5,13},{6,14},{7,15},{8,16},{9,17... | collective-permute-start | bytes 1572872 | tf_op jit(solution)/shard_map/ppermute | solution.py:14
  542.8 2.6 collective-permute-done.12
  545.5 1.5 collective-permute-start.13
  547.0 17.3 %collective-permute-done.29 = f32[32,64,64]{2,1,0:T(8,128)S(1)} collective-permute-done((f32[32,64,64]{2,1,0:T(8,128)S(1)}, f32[32,64,64]{2,1,0:T(8,128)S(1)}, u32[]{:S(2)}, u32[]{:S(2)}) %collective-permute-start.29) | collective-permute-done | bytes 524320 | tf_op jit(solution)/shard_map/ppermute | solution.py:14
  564.4 41.7 %collective-permute-start.30 = (f32[32,64,64]{2,1,0:T(8,128)S(1)}, f32[32,64,64]{2,1,0:T(8,128)S(1)}, u32[]{:S(2)}, u32[]{:S(2)}) collective-permute-start(f32[32,64,64]{2,1,0:T(8,128)S(1)} %multiply_add_fusion.3), channel_id=1, source_target_pairs={{0,16},{1,17},{2,18},{3,19},{4,20},{5,21},{6,22},{7,23},{8,24},{9,... | collective-permute-start | bytes 1572872 | tf_op jit(solution)/shard_map/ppermute | solution.py:14
  607.4 6.8 collective-permute-done.13
  615.7 20.4 %collective-permute-done.30 = f32[32,64,64]{2,1,0:T(8,128)S(1)} collective-permute-done((f32[32,64,64]{2,1,0:T(8,128)S(1)}, f32[32,64,64]{2,1,0:T(8,128)S(1)}, u32[]{:S(2)}, u32[]{:S(2)}) %collective-permute-start.30) | collective-permute-done | bytes 524320 | tf_op jit(solution)/shard_map/ppermute | solution.py:14
  636.3 1.4 collective-permute-start.31
  639.0 9.2 collective-permute-done.14
  649.7 11.0 collective-permute-done.31
  660.8 45.0 %collective-permute-start.32 = (f32[32,64,64]{2,1,0:T(8,128)S(1)}, f32[32,64,64]{2,1,0:T(8,128)S(1)}, u32[]{:S(2)}, u32[]{:S(2)}) collective-permute-start(f32[32,64,64]{2,1,0:T(8,128)S(1)} %multiply_add_fusion.1), channel_id=1, source_target_pairs={{0,64},{1,65},{2,66},{3,67},{4,68},{5,69},{6,70},{7,71},{8,72},{9,... | collective-permute-start | bytes 1572872 | tf_op jit(solution)/shard_map/ppermute | solution.py:14
  705.9 2.1 collective-permute-done.15
  709.4 17.3 %collective-permute-done.32 = f32[32,64,64]{2,1,0:T(8,128)S(1)} collective-permute-done((f32[32,64,64]{2,1,0:T(8,128)S(1)}, f32[32,64,64]{2,1,0:T(8,128)S(1)}, u32[]{:S(2)}, u32[]{:S(2)}) %collective-permute-start.32) | collective-permute-done | bytes 524320 | tf_op jit(solution)/shard_map/ppermute | solution.py:14
  726.9 9.0 collective-permute-start.33
  735.9 18.5 %collective-permute-done.16 = f32[32,64,64]{2,1,0:T(8,128)S(1)} collective-permute-done((f32[32,64,64]{2,1,0:T(8,128)S(1)}, f32[32,64,64]{2,1,0:T(8,128)S(1)}, u32[]{:S(2)}, u32[]{:S(2)}) %collective-permute-start.16) | collective-permute-done | bytes 524320 | tf_op jit(solution)/shard_map/ppermute | solution.py:14
  754.4 2.0 fusion.11
  756.6 2.0 fusion.12
  759.7 2.3 fusion.7
  764.3 334.4 %all-reduce.3.cloned.1.call-done = f32[1024,128]{0,1:T(8,128)} async-done(((f32[1024,128]{0,1:T(8,128)}), f32[1024,128]{0,1:T(8,128)}) %all-reduce.3.cloned.1.call-update) | async-done | bytes 524304
  (99 shorter events, 26.5 us)
Async XLA Ops:
  7.2 350.2 %copy-start = (bf16[128,1024]{1,0:T(8,128)(2,1)S(1)}, bf16[128,1024]{1,0:T(8,128)(2,1)}, u32[]{:S(2)}) copy-start(bf16[128,1024]{1,0:T(8,128)(2,1)} %param.6) | copy-start | bytes 786436
  7.2 349.9 %copy-start.5 = (bf16[128,2048]{1,0:T(8,128)(2,1)S(1)}, bf16[128,2048]{1,0:T(8,128)(2,1)}, u32[]{:S(2)}) copy-start(bf16[128,2048]{1,0:T(8,128)(2,1)} %param.11) | copy-start | bytes 1572868
  7.2 1091.5 %all-reduce.3.cloned.1.call-start = ((), (), s32[]{:S(2)}) async-start(), calls=%async_computation | async-start | bytes 1048576
  8.3 367.1 %collective-permute-start = (f32[32]{0:T(128)S(1)}, f32[32]{0:T(128)S(1)}, u32[]{:S(2)}, u32[]{:S(2)}) collective-permute-start(f32[32]{0:T(128)S(1)} %slice_bitcast_fusion), channel_id=1, source_target_pairs={{1,0},{2,1},{3,2},{4,3},{5,4},{6,5},{7,6},{8,7},{9,8},{10,9},{11,1... | collective-permute-start | bytes 392 | tf_op jit(solution)/shard_map/ppermute | solution.py:14
  11.5 368.4 %collective-permute-start.17 = (f32[32]{0:T(128)S(1)}, f32[32]{0:T(128)S(1)}, u32[]{:S(2)}, u32[]{:S(2)}) collective-permute-start(f32[32]{0:T(128)S(1)} %slice_bitcast_fusion), channel_id=1, source_target_pairs={{0,1},{1,2},{2,3},{3,4},{4,5},{5,6},{6,7},{7,8},{8,9},{9,10},{10,1... | collective-permute-start | bytes 392 | tf_op jit(solution)/shard_map/ppermute | solution.py:14
  357.1 2.5 copy-start.2
  357.4 5.4 copy-start.4
  359.7 3.4 copy-start.6
  359.7 43.2 %collective-permute-start.8 = (f32[32,64,64]{2,1,0:T(8,128)}, f32[32,64,64]{2,1,0:T(8,128)}, u32[]{:S(2)}, u32[]{:S(2)}) collective-permute-start(f32[32,64,64]{2,1,0:T(8,128)} %fusion.19), channel_id=1, source_target_pairs={{1,0},{2,1},{3,2},{4,3},{5,4},{6,5},{7,6},{8,7},{9,8},{10,9},{11,1... | collective-permute-start | bytes 1572872 | tf_op jit(solution)/shard_map/ppermute | solution.py:14
  365.1 47.8 %collective-permute-start.25 = (f32[32,64,64]{2,1,0:T(8,128)}, f32[32,64,64]{2,1,0:T(8,128)S(1)}, u32[]{:S(2)}, u32[]{:S(2)}) collective-permute-start(f32[32,64,64]{2,1,0:T(8,128)} %fusion.22), channel_id=1, source_target_pairs={{0,1},{1,2},{2,3},{3,4},{4,5},{5,6},{6,7},{7,8},{8,9},{9,10},{10,1... | collective-permute-start | bytes 1572872 | tf_op jit(solution)/shard_map/ppermute | solution.py:14
  375.4 6.8 collective-permute-start.1
  380.0 14.6 %collective-permute-start.18 = (f32[32]{0:T(128)S(1)}, f32[32]{0:T(128)S(1)}, u32[]{:S(2)}, u32[]{:S(2)}) collective-permute-start(f32[32]{0:T(128)S(1)} %collective-permute-done.17), channel_id=1, source_target_pairs={{0,1},{1,2},{2,3},{3,4},{4,5},{5,6},{6,7},{7,8},{8,9},{9,10},{10,1... | collective-permute-start | bytes 392 | tf_op jit(solution)/shard_map/ppermute | solution.py:14
  382.2 14.3 %collective-permute-start.2 = (f32[32]{0:T(128)S(1)}, f32[32]{0:T(128)S(1)}, u32[]{:S(2)}, u32[]{:S(2)}) collective-permute-start(f32[32]{0:T(128)S(1)} %get-tuple-element.192), channel_id=1, source_target_pairs={{2,0},{3,1},{4,2},{5,3},{6,4},{7,5},{8,6},{9,7},{10,8},{11,9},{12,... | collective-permute-start | bytes 392 | tf_op jit(solution)/shard_map/ppermute | solution.py:14
  394.6 6.3 collective-permute-start.19
  396.6 8.9 collective-permute-start.3
  401.0 5.8 collective-permute-start.20
  402.9 17.2 %collective-permute-start.9 = (f32[32,64,64]{2,1,0:T(8,128)}, f32[32,64,64]{2,1,0:T(8,128)S(1)}, u32[]{:S(2)}, u32[]{:S(2)}) collective-permute-start(f32[32,64,64]{2,1,0:T(8,128)} %collective-permute-done.8), channel_id=1, source_target_pairs={{1,0},{2,1},{3,2},{4,3},{5,4},{6,5},{7,6},{8,7},{9,8},{10,9},{11,1... | collective-permute-start | bytes 1572872 | tf_op jit(solution)/shard_map/ppermute | solution.py:14
  405.5 9.3 collective-permute-start.4
  406.8 32.0 %collective-permute-start.21 = (f32[32]{0:T(128)S(1)}, f32[32]{0:T(128)S(1)}, u32[]{:S(2)}, u32[]{:S(2)}) collective-permute-start(f32[32]{0:T(128)S(1)} %get-tuple-element.176), channel_id=1, source_target_pairs={{0,8},{1,9},{2,10},{3,11},{4,12},{5,13},{6,14},{7,15},{8,16},{9,17... | collective-permute-start | bytes 392 | tf_op jit(solution)/shard_map/ppermute | solution.py:14
  412.9 23.8 %collective-permute-start.26 = (f32[32,64,64]{2,1,0:T(8,128)S(1)}, f32[32,64,64]{2,1,0:T(8,128)S(1)}, u32[]{:S(2)}, u32[]{:S(2)}) collective-permute-start(f32[32,64,64]{2,1,0:T(8,128)S(1)} %collective-permute-done.25), channel_id=1, source_target_pairs={{0,1},{1,2},{2,3},{3,4},{4,5},{5,6},{6,7},{7,8},{8,9},{9,10},{10,1... | collective-permute-start | bytes 1572872 | tf_op jit(solution)/shard_map/ppermute | solution.py:14
  414.8 81.1 %collective-permute-start.5 = (f32[32]{0:T(128)S(1)}, f32[32]{0:T(128)S(1)}, u32[]{:S(2)}, u32[]{:S(2)}) collective-permute-start(f32[32]{0:T(128)S(1)} %get-tuple-element.186), channel_id=1, source_target_pairs={{16,0},{17,1},{18,2},{19,3},{20,4},{21,5},{22,6},{23,7},{24,8},{25... | collective-permute-start | bytes 392 | tf_op jit(solution)/shard_map/ppermute | solution.py:14
  421.6 28.0 %collective-permute-start.10 = (f32[32,64,64]{2,1,0:T(8,128)S(1)}, f32[32,64,64]{2,1,0:T(8,128)S(1)}, u32[]{:S(2)}, u32[]{:S(2)}) collective-permute-start(f32[32,64,64]{2,1,0:T(8,128)S(1)} %multiply_add_fusion.14), channel_id=1, source_target_pairs={{2,0},{3,1},{4,2},{5,3},{6,4},{7,5},{8,6},{9,7},{10,8},{11,9},{12,... | collective-permute-start | bytes 1572872 | tf_op jit(solution)/shard_map/ppermute | solution.py:14
  436.8 57.0 %collective-permute-start.27 = (f32[32,64,64]{2,1,0:T(8,128)S(1)}, f32[32,64,64]{2,1,0:T(8,128)S(1)}, u32[]{:S(2)}, u32[]{:S(2)}) collective-permute-start(f32[32,64,64]{2,1,0:T(8,128)S(1)} %multiply_add_fusion.6), channel_id=1, source_target_pairs={{0,2},{1,3},{2,4},{3,5},{4,6},{5,7},{6,8},{7,9},{8,10},{9,11},{10,... | collective-permute-start | bytes 1572872 | tf_op jit(solution)/shard_map/ppermute | solution.py:14
  438.8 102.7 %collective-permute-start.22 = (f32[32]{0:T(128)S(1)}, f32[32]{0:T(128)S(1)}, u32[]{:S(2)}, u32[]{:S(2)}) collective-permute-start(f32[32]{0:T(128)S(1)} %get-tuple-element.174), channel_id=1, source_target_pairs={{0,16},{1,17},{2,18},{3,19},{4,20},{5,21},{6,22},{7,23},{8,24},{9,... | collective-permute-start | bytes 392 | tf_op jit(solution)/shard_map/ppermute | solution.py:14
  449.7 47.5 %collective-permute-start.11 = (f32[32,64,64]{2,1,0:T(8,128)S(1)}, f32[32,64,64]{2,1,0:T(8,128)S(1)}, u32[]{:S(2)}, u32[]{:S(2)}) collective-permute-start(f32[32,64,64]{2,1,0:T(8,128)S(1)} %multiply_add_fusion.13), channel_id=1, source_target_pairs={{4,0},{5,1},{6,2},{7,3},{8,4},{9,5},{10,6},{11,7},{12,8},{13,9},{1... | collective-permute-start | bytes 1572872 | tf_op jit(solution)/shard_map/ppermute | solution.py:14
  494.0 26.8 %collective-permute-start.28 = (f32[32,64,64]{2,1,0:T(8,128)S(1)}, f32[32,64,64]{2,1,0:T(8,128)S(1)}, u32[]{:S(2)}, u32[]{:S(2)}) collective-permute-start(f32[32,64,64]{2,1,0:T(8,128)S(1)} %multiply_add_fusion.5), channel_id=1, source_target_pairs={{0,4},{1,5},{2,6},{3,7},{4,8},{5,9},{6,10},{7,11},{8,12},{9,13},{1... | collective-permute-start | bytes 1572872 | tf_op jit(solution)/shard_map/ppermute | solution.py:14
  496.0 110.1 %collective-permute-start.6 = (f32[32]{0:T(128)S(1)}, f32[32]{0:T(128)S(1)}, u32[]{:S(2)}, u32[]{:S(2)}) collective-permute-start(f32[32]{0:T(128)S(1)} %get-tuple-element.184), channel_id=1, source_target_pairs={{32,0},{33,1},{34,2},{35,3},{36,4},{37,5},{38,6},{39,7},{40,8},{41... | collective-permute-start | bytes 392 | tf_op jit(solution)/shard_map/ppermute | solution.py:14
  497.4 47.9 %collective-permute-start.12 = (f32[32,64,64]{2,1,0:T(8,128)S(1)}, f32[32,64,64]{2,1,0:T(8,128)S(1)}, u32[]{:S(2)}, u32[]{:S(2)}) collective-permute-start(f32[32,64,64]{2,1,0:T(8,128)S(1)} %multiply_add_fusion.12), channel_id=1, source_target_pairs={{8,0},{9,1},{10,2},{11,3},{12,4},{13,5},{14,6},{15,7},{16,8},{17,9... | collective-permute-start | bytes 1572872 | tf_op jit(solution)/shard_map/ppermute | solution.py:14
  521.0 43.3 %collective-permute-start.29 = (f32[32,64,64]{2,1,0:T(8,128)S(1)}, f32[32,64,64]{2,1,0:T(8,128)S(1)}, u32[]{:S(2)}, u32[]{:S(2)}) collective-permute-start(f32[32,64,64]{2,1,0:T(8,128)S(1)} %multiply_add_fusion.4), channel_id=1, source_target_pairs={{0,8},{1,9},{2,10},{3,11},{4,12},{5,13},{6,14},{7,15},{8,16},{9,17... | collective-permute-start | bytes 1572872 | tf_op jit(solution)/shard_map/ppermute | solution.py:14
  541.5 96.2 %collective-permute-start.23 = (f32[32]{0:T(128)S(1)}, f32[32]{0:T(128)S(1)}, u32[]{:S(2)}, u32[]{:S(2)}) collective-permute-start(f32[32]{0:T(128)S(1)} %get-tuple-element.172), channel_id=1, source_target_pairs={{0,32},{1,33},{2,34},{3,35},{4,36},{5,37},{6,38},{7,39},{8,40},{9,... | collective-permute-start | bytes 392 | tf_op jit(solution)/shard_map/ppermute | solution.py:14
  545.5 68.8 %collective-permute-start.13 = (f32[32,64,64]{2,1,0:T(8,128)S(1)}, f32[32,64,64]{2,1,0:T(8,128)S(1)}, u32[]{:S(2)}, u32[]{:S(2)}) collective-permute-start(f32[32,64,64]{2,1,0:T(8,128)S(1)} %multiply_add_fusion.11), channel_id=1, source_target_pairs={{16,0},{17,1},{18,2},{19,3},{20,4},{21,5},{22,6},{23,7},{24,8},{25... | collective-permute-start | bytes 1572872 | tf_op jit(solution)/shard_map/ppermute | solution.py:14
  564.4 71.6 %collective-permute-start.30 = (f32[32,64,64]{2,1,0:T(8,128)S(1)}, f32[32,64,64]{2,1,0:T(8,128)S(1)}, u32[]{:S(2)}, u32[]{:S(2)}) collective-permute-start(f32[32,64,64]{2,1,0:T(8,128)S(1)} %multiply_add_fusion.3), channel_id=1, source_target_pairs={{0,16},{1,17},{2,18},{3,19},{4,20},{5,21},{6,22},{7,23},{8,24},{9,... | collective-permute-start | bytes 1572872 | tf_op jit(solution)/shard_map/ppermute | solution.py:14
  606.1 99.7 %collective-permute-start.7 = (f32[32]{0:T(128)S(1)}, f32[32]{0:T(128)S(1)}, u32[]{:S(2)}, u32[]{:S(2)}) collective-permute-start(f32[32]{0:T(128)S(1)} %get-tuple-element.182), channel_id=1, source_target_pairs={{64,0},{65,1},{66,2},{67,3},{68,4},{69,5},{70,6},{71,7},{72,8},{73... | collective-permute-start | bytes 392 | tf_op jit(solution)/shard_map/ppermute | solution.py:14
  614.4 33.8 %collective-permute-start.14 = (f32[32,64,64]{2,1,0:T(8,128)S(1)}, f32[32,64,64]{2,1,0:T(8,128)S(1)}, u32[]{:S(2)}, u32[]{:S(2)}) collective-permute-start(f32[32,64,64]{2,1,0:T(8,128)S(1)} %multiply_add_fusion.10), channel_id=1, source_target_pairs={{32,0},{33,1},{34,2},{35,3},{36,4},{37,5},{38,6},{39,7},{40,8},{41... | collective-permute-start | bytes 1572872 | tf_op jit(solution)/shard_map/ppermute | solution.py:14
  636.3 24.4 %collective-permute-start.31 = (f32[32,64,64]{2,1,0:T(8,128)S(1)}, f32[32,64,64]{2,1,0:T(8,128)S(1)}, u32[]{:S(2)}, u32[]{:S(2)}) collective-permute-start(f32[32,64,64]{2,1,0:T(8,128)S(1)} %multiply_add_fusion.2), channel_id=1, source_target_pairs={{0,32},{1,33},{2,34},{3,35},{4,36},{5,37},{6,38},{7,39},{8,40},{9,... | collective-permute-start | bytes 1572872 | tf_op jit(solution)/shard_map/ppermute | solution.py:14
  637.7 98.2 %collective-permute-start.24 = (f32[32]{0:T(128)S(1)}, f32[32]{0:T(128)S(1)}, u32[]{:S(2)}, u32[]{:S(2)}) collective-permute-start(f32[32]{0:T(128)S(1)} %get-tuple-element.170), channel_id=1, source_target_pairs={{0,64},{1,65},{2,66},{3,67},{4,68},{5,69},{6,70},{7,71},{8,72},{9,... | collective-permute-start | bytes 392 | tf_op jit(solution)/shard_map/ppermute | solution.py:14
  648.4 59.6 %collective-permute-start.15 = (f32[32,64,64]{2,1,0:T(8,128)S(1)}, f32[32,64,64]{2,1,0:T(8,128)S(1)}, u32[]{:S(2)}, u32[]{:S(2)}) collective-permute-start(f32[32,64,64]{2,1,0:T(8,128)S(1)} %multiply_add_fusion.9), channel_id=1, source_target_pairs={{64,0},{65,1},{66,2},{67,3},{68,4},{69,5},{70,6},{71,7},{72,8},{73... | collective-permute-start | bytes 1572872 | tf_op jit(solution)/shard_map/ppermute | solution.py:14
  660.8 65.9 %collective-permute-start.32 = (f32[32,64,64]{2,1,0:T(8,128)S(1)}, f32[32,64,64]{2,1,0:T(8,128)S(1)}, u32[]{:S(2)}, u32[]{:S(2)}) collective-permute-start(f32[32,64,64]{2,1,0:T(8,128)S(1)} %multiply_add_fusion.1), channel_id=1, source_target_pairs={{0,64},{1,65},{2,66},{3,67},{4,68},{5,69},{6,70},{7,71},{8,72},{9,... | collective-permute-start | bytes 1572872 | tf_op jit(solution)/shard_map/ppermute | solution.py:14
  705.9 48.5 %copy-start.8 = (f32[32]{0:T(128)}, f32[32]{0:T(128)S(1)}, u32[]{:S(2)}) copy-start(f32[32]{0:T(128)S(1)} %add_exponential_fusion.1) | copy-start | bytes 388
  708.1 46.3 %collective-permute-start.16 = (f32[32,64,64]{2,1,0:T(8,128)S(1)}, f32[32,64,64]{2,1,0:T(8,128)S(1)}, u32[]{:S(2)}, u32[]{:S(2)}) collective-permute-start(f32[32,64,64]{2,1,0:T(8,128)S(1)} %multiply_add_fusion.8), channel_id=1, source_target_pairs={{128,0},{129,1},{130,2},{131,3},{132,4},{133,5},{134,6},{135,7},{1... | collective-permute-start | bytes 1572872 | tf_op jit(solution)/shard_map/ppermute | solution.py:14
  726.9 29.7 %collective-permute-start.33 = (f32[32,64,64]{2,1,0:T(8,128)S(1)}, f32[32,64,64]{2,1,0:T(8,128)S(1)}, u32[]{:S(2)}, u32[]{:S(2)}) collective-permute-start(f32[32,64,64]{2,1,0:T(8,128)S(1)} %multiply_add_fusion), channel_id=1, source_target_pairs={{0,128},{1,129},{2,130},{3,131},{4,132},{5,133},{6,134},{7,135},{8... | collective-permute-start | bytes 1572872 | tf_op jit(solution)/shard_map/ppermute | solution.py:14
  735.9 20.8 %copy-start.1 = (f32[128,2048]{0,1:T(8,128)S(1)}, f32[128,2048]{0,1:T(8,128)}, u32[]{:S(2)}) copy-start(f32[128,2048]{0,1:T(8,128)} %bitcast_multiply_fusion.1) | copy-start | bytes 3145732
  735.9 20.8 %copy-start.7 = (f32[128,64]{0,1:T(8,128)S(1)}, f32[128,64]{0,1:T(8,128)}, u32[]{:S(2)}) copy-start(f32[128,64]{0,1:T(8,128)} %fusion.44) | copy-start | bytes 98308
  758.6 1.1 copy-start.9
  762.0 1.3 copy-start.3
Sparse Core Ops, SparseCore 0:
  759.8 338.8 all-reduce.2
where the time goes:
time: 1110 us
  waiting for transfers between devices  532 us (48%)
  blocking collectives  344 us (31%)
  starting transfers between devices  188 us (17%)
  matrix products  19.8 us (2%)
  between operations  14.8 us (1%)
    all_gather x1, blocking collectives, per_device(): weights_full = lax.all_gather(w_bc, ('outer', 'inner'), axis=0, tiled=True)  344 us
    unnamed x2, waiting for transfers between devices  334 us
    ppermute x34, waiting for transfers between devices, shifted(): lax.ppermute(value, axis, [(source, source + steps) for source in range(f...  197 us
    ppermute x34, starting transfers between devices, shifted(): lax.ppermute(value, axis, [(source, source + steps) for source in range(f...  188 us
  transfers between devices with their start and end apart: 35, of which 18 were waited for; matrix products, arithmetic and copies ran while one was open for 2% of the time, Pallas kernels for 0%

commit v1 on v0

--- a/solution.py
+++ b/solution.py
@@ -73,7 +73,12 @@
 
 
 def per_device(hidden, x_act, dt_step, log_decay, w_bc, grad_y):
-    weights_full = lax.all_gather(w_bc, ("outer", "inner"), axis=0, tiled=True)
+    weights_full = jnp.concatenate(
+        lax.all_to_all(
+            jnp.stack([w_bc] * lax.axis_size(("outer", "inner"))), ("outer", "inner"), 0, 0
+        ),
+        axis=0,
+    )
     state_width = weights_full.shape[1] // 2
     row_count = hidden.shape[0]
     head_count = dt_step.shape[1]

time: 1110 us -> 817 us (0.74)
  blocking collectives: 344 us -> 0 us
  starting transfers between devices: 188 us -> 242 us
    all_gather x1 -> x0, blocking collectives: 344 us -> none  [per_device(): weights_full = lax.all_gather(w_bc, ('outer', 'inner'), axis=0, tiled=True)]
    ppermute x34, starting transfers between devices: 188 us -> 225 us  [shifted(): lax.ppermute(value, axis, [(source, source + steps) for source in range(f...]
    all_to_all x0 -> x1, starting transfers between devices: none -> 17.2 us  [per_device(): lax.all_to_all(jnp.stack([w_bc] * lax.axis_size(('outer', 'inner'))), ('o...]
    ppermute x34, waiting for transfers between devices: 197 us -> 209 us  [shifted(): lax.ppermute(value, axis, [(source, source + steps) for source in range(f...]
    unnamed x2, waiting for transfers between devices: 334 us -> 323 us
  transfers between devices with their start and end apart: 35 -> 36, of which waited for: 18 -> 17; matrix products, arithmetic and copies ran while one was open for 2% -> 3% of each run, Pallas kernels for 0% -> 0%
where the time goes in v1:
time: 817 us; the launch traced here: 815 us
  waiting for transfers between devices  532 us (65%)
  starting transfers between devices  242 us (30%)
  matrix products  17.2 us (2%)
  between operations  14.9 us (2%)
    unnamed x2, waiting for transfers between devices  323 us
    ppermute x34, starting transfers between devices, shifted(): lax.ppermute(value, axis, [(source, source + steps) for source in range(f...  225 us
    ppermute x34, waiting for transfers between devices, shifted(): lax.ppermute(value, axis, [(source, source + steps) for source in range(f...  209 us
    all_to_all x1, starting transfers between devices, per_device(): lax.all_to_all(jnp.stack([w_bc] * lax.axis_size(('outer', 'inner'))), ('o...  17.2 us
  transfers between devices with their start and end apart: 36, of which 17 were waited for; matrix products, arithmetic and copies ran while one was open for 3% of the time, Pallas kernels for 0%

profile of v1, /device:TPU:2, one launch (start us, length us, event | category | flops | bytes accessed | tf_op | source)
XLA Modules:
  0.0 815.4 jit_solution(3887397964865568706)
XLA Ops:
  8.3 3.4 collective-permute-start
  11.6 1.9 collective-permute-start.17
  13.6 1.5 stack.2
  15.0 17.2 %all-to-all-start = ((bf16[256,4,128]{2,1,0:T(4,128)(2,1)}), bf16[256,4,128]{2,1,0:T(4,128)(2,1)S(1)}, u32[]{:S(2)}, u32[]{:S(2)}) async-start(bf16[256,4,128]{2,1,0:T(4,128)(2,1)} %stack.2), calls=%async_computation | async-start | bytes 524288 | tf_op jit(solution)/shard_map/all_to_all | solution.py:77
  34.1 2.4 fusion
  36.6 3.2 collective-permute-start.1
  39.8 1.9 collective-permute-start.18
  41.8 2.7 collective-permute-start.2
  45.6 2.1 collective-permute-start.19
  47.7 3.2 collective-permute-start.3
  51.9 3.4 collective-permute-start.20
  55.4 1.3 collective-permute-start.4
  57.4 8.5 %collective-permute-start.21 = (f32[32]{0:T(128)S(1)}, f32[32]{0:T(128)S(1)}, u32[]{:S(2)}, u32[]{:S(2)}) collective-permute-start(f32[32]{0:T(128)S(1)} %get-tuple-element.176), channel_id=1, source_target_pairs={{0,8},{1,9},{2,10},{3,11},{4,12},{5,13},{6,14},{7,15},{8,16},{9,17... | collective-permute-start | bytes 392 | tf_op jit(solution)/shard_map/ppermute | solution.py:14
  67.1 1.9 collective-permute-start.8
  69.1 1.3 collective-permute-start.5
  71.4 2.4 collective-permute-start.25
  73.8 9.1 %collective-permute-start.22 = (f32[32]{0:T(128)S(1)}, f32[32]{0:T(128)S(1)}, u32[]{:S(2)}, u32[]{:S(2)}) collective-permute-start(f32[32]{0:T(128)S(1)} %get-tuple-element.174), channel_id=1, source_target_pairs={{0,16},{1,17},{2,18},{3,19},{4,20},{5,21},{6,22},{7,23},{8,24},{9,... | collective-permute-start | bytes 392 | tf_op jit(solution)/shard_map/ppermute | solution.py:14
  82.9 4.0 collective-permute-done.8
  87.0 4.7 collective-permute-start.9
  93.0 12.6 %collective-permute-start.23 = (f32[32]{0:T(128)S(1)}, f32[32]{0:T(128)S(1)}, u32[]{:S(2)}, u32[]{:S(2)}) collective-permute-start(f32[32]{0:T(128)S(1)} %get-tuple-element.172), channel_id=1, source_target_pairs={{0,32},{1,33},{2,34},{3,35},{4,36},{5,37},{6,38},{7,39},{8,40},{9,... | collective-permute-start | bytes 392 | tf_op jit(solution)/shard_map/ppermute | solution.py:14
  105.6 1.9 collective-permute-start.26
  107.5 7.2 collective-permute-done.6
  116.2 3.2 collective-permute-start.10
  119.3 5.0 collective-permute-done.26
  124.5 1.9 collective-permute-start.27
  126.5 11.9 %collective-permute-start.24 = (f32[32]{0:T(128)S(1)}, f32[32]{0:T(128)S(1)}, u32[]{:S(2)}, u32[]{:S(2)}) collective-permute-start(f32[32]{0:T(128)S(1)} %get-tuple-element.170), channel_id=1, source_target_pairs={{0,64},{1,65},{2,66},{3,67},{4,68},{5,69},{6,70},{7,71},{8,72},{9,... | collective-permute-start | bytes 392 | tf_op jit(solution)/shard_map/ppermute | solution.py:14
  138.4 5.7 collective-permute-done.10
  144.3 1.9 collective-permute-start.11
  146.3 42.1 %collective-permute-done.27 = f32[32,64,64]{2,1,0:T(8,128)S(1)} collective-permute-done((f32[32,64,64]{2,1,0:T(8,128)S(1)}, f32[32,64,64]{2,1,0:T(8,128)S(1)}, u32[]{:S(2)}, u32[]{:S(2)}) %collective-permute-start.27) | collective-permute-done | bytes 524320 | tf_op jit(solution)/shard_map/ppermute | solution.py:14
  188.5 1.9 collective-permute-start.28
  192.0 27.3 %collective-permute-done.28 = f32[32,64,64]{2,1,0:T(8,128)S(1)} collective-permute-done((f32[32,64,64]{2,1,0:T(8,128)S(1)}, f32[32,64,64]{2,1,0:T(8,128)S(1)}, u32[]{:S(2)}, u32[]{:S(2)}) %collective-permute-start.28) | collective-permute-done | bytes 524320 | tf_op jit(solution)/shard_map/ppermute | solution.py:14
  219.5 1.4 collective-permute-start.29
  222.4 21.7 %collective-permute-done.29 = f32[32,64,64]{2,1,0:T(8,128)S(1)} collective-permute-done((f32[32,64,64]{2,1,0:T(8,128)S(1)}, f32[32,64,64]{2,1,0:T(8,128)S(1)}, u32[]{:S(2)}, u32[]{:S(2)}) %collective-permute-start.29) | collective-permute-done | bytes 524320 | tf_op jit(solution)/shard_map/ppermute | solution.py:14
  244.3 3.1 collective-permute-start.30
  249.1 10.5 %collective-permute-done.30 = f32[32,64,64]{2,1,0:T(8,128)S(1)} collective-permute-done((f32[32,64,64]{2,1,0:T(8,128)S(1)}, f32[32,64,64]{2,1,0:T(8,128)S(1)}, u32[]{:S(2)}, u32[]{:S(2)}) %collective-permute-start.30) | collective-permute-done | bytes 524320 | tf_op jit(solution)/shard_map/ppermute | solution.py:14
  259.7 61.1 %collective-permute-start.31 = (f32[32,64,64]{2,1,0:T(8,128)S(1)}, f32[32,64,64]{2,1,0:T(8,128)S(1)}, u32[]{:S(2)}, u32[]{:S(2)}) collective-permute-start(f32[32,64,64]{2,1,0:T(8,128)S(1)} %multiply_add_fusion.2), channel_id=1, source_target_pairs={{0,32},{1,33},{2,34},{3,35},{4,36},{5,37},{6,38},{7,39},{8,40},{9,... | collective-permute-start | bytes 1572872 | tf_op jit(solution)/shard_map/ppermute | solution.py:14
  320.8 3.5 fusion.3
  324.3 10.6 %collective-permute-done.14 = f32[32,64,64]{2,1,0:T(8,128)S(1)} collective-permute-done((f32[32,64,64]{2,1,0:T(8,128)S(1)}, f32[32,64,64]{2,1,0:T(8,128)S(1)}, u32[]{:S(2)}, u32[]{:S(2)}) %collective-permute-start.14) | collective-permute-done | bytes 524320 | tf_op jit(solution)/shard_map/ppermute | solution.py:14
  336.4 31.2 %collective-permute-done.31 = f32[32,64,64]{2,1,0:T(8,128)S(1)} collective-permute-done((f32[32,64,64]{2,1,0:T(8,128)S(1)}, f32[32,64,64]{2,1,0:T(8,128)S(1)}, u32[]{:S(2)}, u32[]{:S(2)}) %collective-permute-start.31) | collective-permute-done | bytes 524320 | tf_op jit(solution)/shard_map/ppermute | solution.py:14
  367.8 52.0 %collective-permute-start.32 = (f32[32,64,64]{2,1,0:T(8,128)S(1)}, f32[32,64,64]{2,1,0:T(8,128)S(1)}, u32[]{:S(2)}, u32[]{:S(2)}) collective-permute-start(f32[32,64,64]{2,1,0:T(8,128)S(1)} %multiply_add_fusion.1), channel_id=1, source_target_pairs={{0,64},{1,65},{2,66},{3,67},{4,68},{5,69},{6,70},{7,71},{8,72},{9,... | collective-permute-start | bytes 1572872 | tf_op jit(solution)/shard_map/ppermute | solution.py:14
  421.6 21.1 %collective-permute-done.32 = f32[32,64,64]{2,1,0:T(8,128)S(1)} collective-permute-done((f32[32,64,64]{2,1,0:T(8,128)S(1)}, f32[32,64,64]{2,1,0:T(8,128)S(1)}, u32[]{:S(2)}, u32[]{:S(2)}) %collective-permute-start.32) | collective-permute-done | bytes 524320 | tf_op jit(solution)/shard_map/ppermute | solution.py:14
  442.8 11.7 %collective-permute-start.33 = (f32[32,64,64]{2,1,0:T(8,128)S(1)}, f32[32,64,64]{2,1,0:T(8,128)S(1)}, u32[]{:S(2)}, u32[]{:S(2)}) collective-permute-start(f32[32,64,64]{2,1,0:T(8,128)S(1)} %multiply_add_fusion), channel_id=1, source_target_pairs={{0,128},{1,129},{2,130},{3,131},{4,132},{5,133},{6,134},{7,135},{8... | collective-permute-start | bytes 1572872 | tf_op jit(solution)/shard_map/ppermute | solution.py:14
  454.7 18.4 %collective-permute-done.16 = f32[32,64,64]{2,1,0:T(8,128)S(1)} collective-permute-done((f32[32,64,64]{2,1,0:T(8,128)S(1)}, f32[32,64,64]{2,1,0:T(8,128)S(1)}, u32[]{:S(2)}, u32[]{:S(2)}) %collective-permute-start.16) | collective-permute-done | bytes 524320 | tf_op jit(solution)/shard_map/ppermute | solution.py:14
  473.1 2.0 fusion.11
  476.2 2.0 fusion.12
  479.3 2.3 fusion.7
  481.6 1.3 copy.49
  483.9 323.1 %all-reduce.3.cloned.1.call-done = f32[1024,128]{0,1:T(8,128)} async-done(((f32[1024,128]{0,1:T(8,128)}), f32[1024,128]{0,1:T(8,128)}) %all-reduce.3.cloned.1.call-update) | async-done | bytes 524304
  (107 shorter events, 25.1 us)
Async XLA Ops:
  7.2 58.7 %copy-start = (bf16[128,1024]{1,0:T(8,128)(2,1)S(1)}, bf16[128,1024]{1,0:T(8,128)(2,1)}, u32[]{:S(2)}) copy-start(bf16[128,1024]{1,0:T(8,128)(2,1)} %param.6) | copy-start | bytes 786436
  7.2 25.2 %copy-start.5 = (bf16[128,2048]{1,0:T(8,128)(2,1)S(1)}, bf16[128,2048]{1,0:T(8,128)(2,1)}, u32[]{:S(2)}) copy-start(bf16[128,2048]{1,0:T(8,128)(2,1)} %param.11) | copy-start | bytes 1572868
  8.3 24.5 %copy-start.4 = (bf16[128,2048]{1,0:T(8,128)(2,1)S(1)}, bf16[128,2048]{1,0:T(8,128)(2,1)}, u32[]{:S(2)}) copy-start(bf16[128,2048]{1,0:T(8,128)(2,1)} %param.7) | copy-start | bytes 1572868
  8.3 28.3 %collective-permute-start = (f32[32]{0:T(128)S(1)}, f32[32]{0:T(128)S(1)}, u32[]{:S(2)}, u32[]{:S(2)}) collective-permute-start(f32[32]{0:T(128)S(1)} %slice_bitcast_fusion), channel_id=1, source_target_pairs={{1,0},{2,1},{3,2},{4,3},{5,4},{6,5},{7,6},{8,7},{9,8},{10,9},{11,1... | collective-permute-start | bytes 392 | tf_op jit(solution)/shard_map/ppermute | solution.py:14
  11.6 28.2 %collective-permute-start.17 = (f32[32]{0:T(128)S(1)}, f32[32]{0:T(128)S(1)}, u32[]{:S(2)}, u32[]{:S(2)}) collective-permute-start(f32[32]{0:T(128)S(1)} %slice_bitcast_fusion), channel_id=1, source_target_pairs={{0,1},{1,2},{2,3},{3,4},{4,5},{5,6},{6,7},{7,8},{8,9},{9,10},{10,1... | collective-permute-start | bytes 392 | tf_op jit(solution)/shard_map/ppermute | solution.py:14
  15.0 50.8 %all-to-all-start = ((bf16[256,4,128]{2,1,0:T(4,128)(2,1)}), bf16[256,4,128]{2,1,0:T(4,128)(2,1)S(1)}, u32[]{:S(2)}, u32[]{:S(2)}) async-start(bf16[256,4,128]{2,1,0:T(4,128)(2,1)} %stack.2), calls=%async_computation | async-start | bytes 524288 | tf_op jit(solution)/shard_map/all_to_all | solution.py:77
  32.2 774.8 %all-reduce.3.cloned.1.call-start = ((), (), s32[]{:S(2)}) async-start(), calls=%async_computation.1 | async-start | bytes 1048576
  32.3 1.8 copy-start.9
  33.0 1.2 copy-start.6
  36.6 5.2 collective-permute-start.1
  39.8 5.8 collective-permute-start.18
  41.8 5.9 collective-permute-start.2
  45.6 6.3 collective-permute-start.19
  47.7 7.6 collective-permute-start.3
  51.9 5.4 collective-permute-start.20
  55.4 13.7 %collective-permute-start.4 = (f32[32]{0:T(128)S(1)}, f32[32]{0:T(128)S(1)}, u32[]{:S(2)}, u32[]{:S(2)}) collective-permute-start(f32[32]{0:T(128)S(1)} %get-tuple-element.188), channel_id=1, source_target_pairs={{8,0},{9,1},{10,2},{11,3},{12,4},{13,5},{14,6},{15,7},{16,8},{17,9... | collective-permute-start | bytes 392 | tf_op jit(solution)/shard_map/ppermute | solution.py:14
  57.4 16.4 %collective-permute-start.21 = (f32[32]{0:T(128)S(1)}, f32[32]{0:T(128)S(1)}, u32[]{:S(2)}, u32[]{:S(2)}) collective-permute-start(f32[32]{0:T(128)S(1)} %get-tuple-element.176), channel_id=1, source_target_pairs={{0,8},{1,9},{2,10},{3,11},{4,12},{5,13},{6,14},{7,15},{8,16},{9,17... | collective-permute-start | bytes 392 | tf_op jit(solution)/shard_map/ppermute | solution.py:14
  65.9 1.3 copy-start.2
  67.1 19.8 %collective-permute-start.8 = (f32[32,64,64]{2,1,0:T(8,128)S(1)}, f32[32,64,64]{2,1,0:T(8,128)S(1)}, u32[]{:S(2)}, u32[]{:S(2)}) collective-permute-start(f32[32,64,64]{2,1,0:T(8,128)S(1)} %fusion.19), channel_id=1, source_target_pairs={{1,0},{2,1},{3,2},{4,3},{5,4},{6,5},{7,6},{8,7},{9,8},{10,9},{11,1... | collective-permute-start | bytes 1572872 | tf_op jit(solution)/shard_map/ppermute | solution.py:14
  69.1 22.6 %collective-permute-start.5 = (f32[32]{0:T(128)S(1)}, f32[32]{0:T(128)S(1)}, u32[]{:S(2)}, u32[]{:S(2)}) collective-permute-start(f32[32]{0:T(128)S(1)} %get-tuple-element.186), channel_id=1, source_target_pairs={{16,0},{17,1},{18,2},{19,3},{20,4},{21,5},{22,6},{23,7},{24,8},{25... | collective-permute-start | bytes 392 | tf_op jit(solution)/shard_map/ppermute | solution.py:14
  71.4 34.2 %collective-permute-start.25 = (f32[32,64,64]{2,1,0:T(8,128)S(1)}, f32[32,64,64]{2,1,0:T(8,128)S(1)}, u32[]{:S(2)}, u32[]{:S(2)}) collective-permute-start(f32[32,64,64]{2,1,0:T(8,128)S(1)} %fusion.22), channel_id=1, source_target_pairs={{0,1},{1,2},{2,3},{3,4},{4,5},{5,6},{6,7},{7,8},{8,9},{9,10},{10,1... | collective-permute-start | bytes 1572872 | tf_op jit(solution)/shard_map/ppermute | solution.py:14
  73.8 19.2 %collective-permute-start.22 = (f32[32]{0:T(128)S(1)}, f32[32]{0:T(128)S(1)}, u32[]{:S(2)}, u32[]{:S(2)}) collective-permute-start(f32[32]{0:T(128)S(1)} %get-tuple-element.174), channel_id=1, source_target_pairs={{0,16},{1,17},{2,18},{3,19},{4,20},{5,21},{6,22},{7,23},{8,24},{9,... | collective-permute-start | bytes 392 | tf_op jit(solution)/shard_map/ppermute | solution.py:14
  87.0 29.1 %collective-permute-start.9 = (f32[32,64,64]{2,1,0:T(8,128)S(1)}, f32[32,64,64]{2,1,0:T(8,128)S(1)}, u32[]{:S(2)}, u32[]{:S(2)}) collective-permute-start(f32[32,64,64]{2,1,0:T(8,128)S(1)} %collective-permute-done.8), channel_id=1, source_target_pairs={{1,0},{2,1},{3,2},{4,3},{5,4},{6,5},{7,6},{8,7},{9,8},{10,9},{11,1... | collective-permute-start | bytes 1572872 | tf_op jit(solution)/shard_map/ppermute | solution.py:14
  91.7 23.0 %collective-permute-start.6 = (f32[32]{0:T(128)S(1)}, f32[32]{0:T(128)S(1)}, u32[]{:S(2)}, u32[]{:S(2)}) collective-permute-start(f32[32]{0:T(128)S(1)} %get-tuple-element.184), channel_id=1, source_target_pairs={{32,0},{33,1},{34,2},{35,3},{36,4},{37,5},{38,6},{39,7},{40,8},{41... | collective-permute-start | bytes 392 | tf_op jit(solution)/shard_map/ppermute | solution.py:14
  93.0 33.4 %collective-permute-start.23 = (f32[32]{0:T(128)S(1)}, f32[32]{0:T(128)S(1)}, u32[]{:S(2)}, u32[]{:S(2)}) collective-permute-start(f32[32]{0:T(128)S(1)} %get-tuple-element.172), channel_id=1, source_target_pairs={{0,32},{1,33},{2,34},{3,35},{4,36},{5,37},{6,38},{7,39},{8,40},{9,... | collective-permute-start | bytes 392 | tf_op jit(solution)/shard_map/ppermute | solution.py:14
  105.6 18.7 %collective-permute-start.26 = (f32[32,64,64]{2,1,0:T(8,128)S(1)}, f32[32,64,64]{2,1,0:T(8,128)S(1)}, u32[]{:S(2)}, u32[]{:S(2)}) collective-permute-start(f32[32,64,64]{2,1,0:T(8,128)S(1)} %collective-permute-done.25), channel_id=1, source_target_pairs={{0,1},{1,2},{2,3},{3,4},{4,5},{5,6},{6,7},{7,8},{8,9},{9,10},{10,1... | collective-permute-start | bytes 1572872 | tf_op jit(solution)/shard_map/ppermute | solution.py:14
  114.7 75.8 %collective-permute-start.7 = (f32[32]{0:T(128)S(1)}, f32[32]{0:T(128)S(1)}, u32[]{:S(2)}, u32[]{:S(2)}) collective-permute-start(f32[32]{0:T(128)S(1)} %get-tuple-element.182), channel_id=1, source_target_pairs={{64,0},{65,1},{66,2},{67,3},{68,4},{69,5},{70,6},{71,7},{72,8},{73... | collective-permute-start | bytes 392 | tf_op jit(solution)/shard_map/ppermute | solution.py:14
  116.2 28.0 %collective-permute-start.10 = (f32[32,64,64]{2,1,0:T(8,128)S(1)}, f32[32,64,64]{2,1,0:T(8,128)S(1)}, u32[]{:S(2)}, u32[]{:S(2)}) collective-permute-start(f32[32,64,64]{2,1,0:T(8,128)S(1)} %multiply_add_fusion.14), channel_id=1, source_target_pairs={{2,0},{3,1},{4,2},{5,3},{6,4},{7,5},{8,6},{9,7},{10,8},{11,9},{12,... | collective-permute-start | bytes 1572872 | tf_op jit(solution)/shard_map/ppermute | solution.py:14
  124.5 63.8 %collective-permute-start.27 = (f32[32,64,64]{2,1,0:T(8,128)S(1)}, f32[32,64,64]{2,1,0:T(8,128)S(1)}, u32[]{:S(2)}, u32[]{:S(2)}) collective-permute-start(f32[32,64,64]{2,1,0:T(8,128)S(1)} %multiply_add_fusion.6), channel_id=1, source_target_pairs={{0,2},{1,3},{2,4},{3,5},{4,6},{5,7},{6,8},{7,9},{8,10},{9,11},{10,... | collective-permute-start | bytes 1572872 | tf_op jit(solution)/shard_map/ppermute | solution.py:14
  126.5 94.4 %collective-permute-start.24 = (f32[32]{0:T(128)S(1)}, f32[32]{0:T(128)S(1)}, u32[]{:S(2)}, u32[]{:S(2)}) collective-permute-start(f32[32]{0:T(128)S(1)} %get-tuple-element.170), channel_id=1, source_target_pairs={{0,64},{1,65},{2,66},{3,67},{4,68},{5,69},{6,70},{7,71},{8,72},{9,... | collective-permute-start | bytes 392 | tf_op jit(solution)/shard_map/ppermute | solution.py:14
  144.3 46.2 %collective-permute-start.11 = (f32[32,64,64]{2,1,0:T(8,128)S(1)}, f32[32,64,64]{2,1,0:T(8,128)S(1)}, u32[]{:S(2)}, u32[]{:S(2)}) collective-permute-start(f32[32,64,64]{2,1,0:T(8,128)S(1)} %multiply_add_fusion.13), channel_id=1, source_target_pairs={{4,0},{5,1},{6,2},{7,3},{8,4},{9,5},{10,6},{11,7},{12,8},{13,9},{1... | collective-permute-start | bytes 1572872 | tf_op jit(solution)/shard_map/ppermute | solution.py:14
  188.5 30.8 %collective-permute-start.28 = (f32[32,64,64]{2,1,0:T(8,128)S(1)}, f32[32,64,64]{2,1,0:T(8,128)S(1)}, u32[]{:S(2)}, u32[]{:S(2)}) collective-permute-start(f32[32,64,64]{2,1,0:T(8,128)S(1)} %multiply_add_fusion.5), channel_id=1, source_target_pairs={{0,4},{1,5},{2,6},{3,7},{4,8},{5,9},{6,10},{7,11},{8,12},{9,13},{1... | collective-permute-start | bytes 1572872 | tf_op jit(solution)/shard_map/ppermute | solution.py:14
  190.5 282.6 %copy-start.11 = (f32[32]{0:T(128)}, f32[32]{0:T(128)S(1)}, u32[]{:S(2)}) copy-start(f32[32]{0:T(128)S(1)} %add_exponential_fusion.1) | copy-start | bytes 388
  190.7 30.2 %collective-permute-start.12 = (f32[32,64,64]{2,1,0:T(8,128)S(1)}, f32[32,64,64]{2,1,0:T(8,128)S(1)}, u32[]{:S(2)}, u32[]{:S(2)}) collective-permute-start(f32[32,64,64]{2,1,0:T(8,128)S(1)} %multiply_add_fusion.12), channel_id=1, source_target_pairs={{8,0},{9,1},{10,2},{11,3},{12,4},{13,5},{14,6},{15,7},{16,8},{17,9... | collective-permute-start | bytes 1572872 | tf_op jit(solution)/shard_map/ppermute | solution.py:14
  219.5 24.6 %collective-permute-start.29 = (f32[32,64,64]{2,1,0:T(8,128)S(1)}, f32[32,64,64]{2,1,0:T(8,128)S(1)}, u32[]{:S(2)}, u32[]{:S(2)}) collective-permute-start(f32[32,64,64]{2,1,0:T(8,128)S(1)} %multiply_add_fusion.4), channel_id=1, source_target_pairs={{0,8},{1,9},{2,10},{3,11},{4,12},{5,13},{6,14},{7,15},{8,16},{9,17... | collective-permute-start | bytes 1572872 | tf_op jit(solution)/shard_map/ppermute | solution.py:14
  221.1 26.6 %collective-permute-start.13 = (f32[32,64,64]{2,1,0:T(8,128)S(1)}, f32[32,64,64]{2,1,0:T(8,128)S(1)}, u32[]{:S(2)}, u32[]{:S(2)}) collective-permute-start(f32[32,64,64]{2,1,0:T(8,128)S(1)} %multiply_add_fusion.11), channel_id=1, source_target_pairs={{16,0},{17,1},{18,2},{19,3},{20,4},{21,5},{22,6},{23,7},{24,8},{25... | collective-permute-start | bytes 1572872 | tf_op jit(solution)/shard_map/ppermute | solution.py:14
  244.3 15.3 %collective-permute-start.30 = (f32[32,64,64]{2,1,0:T(8,128)S(1)}, f32[32,64,64]{2,1,0:T(8,128)S(1)}, u32[]{:S(2)}, u32[]{:S(2)}) collective-permute-start(f32[32,64,64]{2,1,0:T(8,128)S(1)} %multiply_add_fusion.3), channel_id=1, source_target_pairs={{0,16},{1,17},{2,18},{3,19},{4,20},{5,21},{6,22},{7,23},{8,24},{9,... | collective-permute-start | bytes 1572872 | tf_op jit(solution)/shard_map/ppermute | solution.py:14
  247.8 87.1 %collective-permute-start.14 = (f32[32,64,64]{2,1,0:T(8,128)S(1)}, f32[32,64,64]{2,1,0:T(8,128)S(1)}, u32[]{:S(2)}, u32[]{:S(2)}) collective-permute-start(f32[32,64,64]{2,1,0:T(8,128)S(1)} %multiply_add_fusion.10), channel_id=1, source_target_pairs={{32,0},{33,1},{34,2},{35,3},{36,4},{37,5},{38,6},{39,7},{40,8},{41... | collective-permute-start | bytes 1572872 | tf_op jit(solution)/shard_map/ppermute | solution.py:14
  259.6 61.3 %copy-start.10 = (pred[128,128]{0,1:T(8,128)(4,1)S(1)}, pred[128,128]{0,1:T(8,128)(4,1)}, u32[]{:S(2)}) copy-start(pred[128,128]{0,1:T(8,128)(4,1)} %copy-done.9) | copy-start | bytes 49156
  259.7 107.9 %collective-permute-start.31 = (f32[32,64,64]{2,1,0:T(8,128)S(1)}, f32[32,64,64]{2,1,0:T(8,128)S(1)}, u32[]{:S(2)}, u32[]{:S(2)}) collective-permute-start(f32[32,64,64]{2,1,0:T(8,128)S(1)} %multiply_add_fusion.2), channel_id=1, source_target_pairs={{0,32},{1,33},{2,34},{3,35},{4,36},{5,37},{6,38},{7,39},{8,40},{9,... | collective-permute-start | bytes 1572872 | tf_op jit(solution)/shard_map/ppermute | solution.py:14
  335.1 85.0 %collective-permute-start.15 = (f32[32,64,64]{2,1,0:T(8,128)S(1)}, f32[32,64,64]{2,1,0:T(8,128)S(1)}, u32[]{:S(2)}, u32[]{:S(2)}) collective-permute-start(f32[32,64,64]{2,1,0:T(8,128)S(1)} %multiply_add_fusion.9), channel_id=1, source_target_pairs={{64,0},{65,1},{66,2},{67,3},{68,4},{69,5},{70,6},{71,7},{72,8},{73... | collective-permute-start | bytes 1572872 | tf_op jit(solution)/shard_map/ppermute | solution.py:14
  367.8 74.9 %collective-permute-start.32 = (f32[32,64,64]{2,1,0:T(8,128)S(1)}, f32[32,64,64]{2,1,0:T(8,128)S(1)}, u32[]{:S(2)}, u32[]{:S(2)}) collective-permute-start(f32[32,64,64]{2,1,0:T(8,128)S(1)} %multiply_add_fusion.1), channel_id=1, source_target_pairs={{0,64},{1,65},{2,66},{3,67},{4,68},{5,69},{6,70},{7,71},{8,72},{9,... | collective-permute-start | bytes 1572872 | tf_op jit(solution)/shard_map/ppermute | solution.py:14
  420.3 52.8 %collective-permute-start.16 = (f32[32,64,64]{2,1,0:T(8,128)S(1)}, f32[32,64,64]{2,1,0:T(8,128)S(1)}, u32[]{:S(2)}, u32[]{:S(2)}) collective-permute-start(f32[32,64,64]{2,1,0:T(8,128)S(1)} %multiply_add_fusion.8), channel_id=1, source_target_pairs={{128,0},{129,1},{130,2},{131,3},{132,4},{133,5},{134,6},{135,7},{1... | collective-permute-start | bytes 1572872 | tf_op jit(solution)/shard_map/ppermute | solution.py:14
  442.6 30.5 %copy-start.7 = (f32[128,32]{0,1:T(8,128)S(1)}, f32[128,32]{0,1:T(8,128)}, u32[]{:S(2)}) copy-start(f32[128,32]{0,1:T(8,128)} %param.8) | copy-start | bytes 49156
  442.8 33.4 %collective-permute-start.33 = (f32[32,64,64]{2,1,0:T(8,128)S(1)}, f32[32,64,64]{2,1,0:T(8,128)S(1)}, u32[]{:S(2)}, u32[]{:S(2)}) collective-permute-start(f32[32,64,64]{2,1,0:T(8,128)S(1)} %multiply_add_fusion), channel_id=1, source_target_pairs={{0,128},{1,129},{2,130},{3,131},{4,132},{5,133},{6,134},{7,135},{8... | collective-permute-start | bytes 1572872 | tf_op jit(solution)/shard_map/ppermute | solution.py:14
  454.7 21.5 %copy-start.1 = (f32[128,2048]{0,1:T(8,128)S(1)}, f32[128,2048]{0,1:T(8,128)}, u32[]{:S(2)}) copy-start(f32[128,2048]{0,1:T(8,128)} %bitcast_multiply_fusion.1) | copy-start | bytes 3145732
  478.2 1.1 copy-start.8
  481.5 1.3 copy-start.3
  (1 other events, 1.1 us)
Sparse Core Ops, SparseCore 0:
  479.4 327.5 all-reduce.2
